TPU v7x, 128 devices: a whole 4x4x4 slice. The times are simulated.
128 devices in a mesh: frame: 16 (over x_hi, z, core), head: 8 (over y, x_lo).
Axes of the slice: x: 4 (x_hi: 2, x_lo: 2; x = x_hi * 2 + x_lo), y: 4, z: 4, core: 2. Of those that a mesh axis runs over, the one named last changes fastest.
Arguments:
- latents: bfloat16 [64, 128, 5120], P('frame'), may hold values from -6 to 6
- levels: int32 [64], P('frame'), may hold values from 0 to 49
- mod_table: float32 [50, 3, 5120], replicated, may hold values from -3 to 3
- w_query: bfloat16 [5120, 3072], P(None, 'head')
- w_key: bfloat16 [5120, 3072], P(None, 'head')
- w_value: bfloat16 [5120, 3072], P(None, 'head'), may hold values from -0.078125 to 0.078125
- w_out: bfloat16 [3072, 5120], P('head'), may hold values from -0.109375 to 0.109375
- query_gain: float32 [3072], P('head'), may hold values from 0.5 to 5
- key_gain: float32 [3072], P('head'), may hold values from 0.5 to 5
Outputs:
- advanced: bfloat16 [64, 128, 5120], P('frame', None, 'head')
All inputs are finite; a program needn't handle non-finite values.
Results may differ from a plain program's by a relative error of at most 0.0055.
Values may be sent and summed in bfloat16 or wider, within the bound.
A program may use at most 128 MiB of HBM per device.

v0:
```python
import jax
import jax.numpy as jnp
from jax import lax
from jax.sharding import PartitionSpec as P

HS = 128


def shifted(value, axis, steps):
    count = lax.axis_size(axis)
    pairs = [(source, (source + steps) % count) for source in range(count)]
    return lax.ppermute(value, axis, pairs)


def attend(queries, key_rows, value_rows):
    scores = jnp.einsum(
        "fphd,gphd->phfg", queries, key_rows, preferred_element_type=jnp.float32
    ) * (1.0 / HS**0.5)
    largest = jnp.max(scores, axis=-1, keepdims=True)
    powers = jnp.exp(scores - largest)
    totals = jnp.sum(powers, axis=-1)
    rounded = powers.astype(jnp.bfloat16)
    numerator = jnp.einsum(
        "phfg,gphd->fphd", rounded, value_rows, preferred_element_type=jnp.float32
    )
    return (numerator / jnp.transpose(totals, (2, 0, 1))[..., None]).astype(jnp.bfloat16)


def on_device(latents, levels, mod_table, w_query, w_key, w_value, w_out, query_gain, key_gain):
    frames_dev, positions, model_width = latents.shape
    level_count = mod_table.shape[0]
    heads_dev = w_query.shape[1] // HS
    flat_rows = frames_dev * positions
    selector = (levels[:, None] == jnp.arange(level_count, dtype=jnp.int32)[None, :]).astype(
        jnp.float32
    )
    modulation = jnp.dot(
        selector,
        mod_table.reshape(level_count, 3 * model_width),
        precision=lax.Precision.HIGHEST,
        preferred_element_type=jnp.float32,
    ).reshape(frames_dev, 3, model_width)
    source = latents.astype(jnp.float32)
    average = jnp.mean(source, axis=-1, keepdims=True)
    centred = source - average
    variance = jnp.mean(centred * centred, axis=-1, keepdims=True)
    normed = centred * lax.rsqrt(variance + 1e-06)
    hidden = (normed * (1.0 + modulation[:, 1][:, None, :]) + modulation[:, 0][:, None, :]).astype(
        jnp.bfloat16
    )
    flat = hidden.reshape(flat_rows, model_width)

    def normed_heads(weight, gain):
        projected = jnp.dot(flat, weight, preferred_element_type=jnp.float32).reshape(
            frames_dev, positions, heads_dev, HS
        )
        power = jnp.mean(projected * projected, axis=-1, keepdims=True)
        return (projected * lax.rsqrt(power + 1e-06) * gain.reshape(heads_dev, HS)).astype(
            jnp.bfloat16
        )

    queries = normed_heads(w_query, query_gain)
    key_rows = normed_heads(w_key, key_gain)
    value_rows = (
        jnp.dot(flat, w_value, preferred_element_type=jnp.float32)
        .astype(jnp.bfloat16)
        .reshape(frames_dev, positions, heads_dev, HS)
    )
    all_keys, all_values = (
        lax.all_gather(key_rows, "frame", axis=0, tiled=True),
        lax.all_gather(value_rows, "frame", axis=0, tiled=True),
    )
    attended = attend(queries, all_keys, all_values)
    partial_sum = jnp.dot(
        attended.reshape(flat_rows, heads_dev * HS), w_out, preferred_element_type=jnp.float32
    ).reshape(frames_dev, positions, model_width)
    summed = lax.psum_scatter(partial_sum, "head", scatter_dimension=2, tiled=True)
    columns = summed.shape[2]
    offset = lax.axis_index("head") * columns
    residual_cols = lax.dynamic_slice_in_dim(source, offset, columns, 2)
    gating = lax.dynamic_slice_in_dim(modulation[:, 2], offset, columns, 1)
    block_out = (residual_cols + gating[:, None, :] * summed).astype(jnp.bfloat16)
    return shifted(block_out, "frame", 1)


def solution(mesh):
    return jax.shard_map(
        on_device,
        mesh=mesh,
        in_specs=(
            P("frame", None, None),
            P("frame"),
            P(),
            P(None, "head"),
            P(None, "head"),
            P(None, "head"),
            P("head", None),
            P("head"),
            P("head"),
        ),
        out_specs=P("frame", None, "head"),
        check_vma=False,
    )
```

profile of v0, /device:TPU:6, one launch (start us, length us, event | category | flops | bytes accessed | tf_op | source)
XLA Modules:
  0.0 428.2 jit_solution(11186911043544773899)
XLA Ops:
  6.5 4.1 copy.25
  11.5 3.7 copy.41
  15.2 5.9 %dot_general.36 = f32[3,5120,50]{1,0,2:T(4,128)} reshape(f32[15360,50]{0,1:T(8,128)} %bitcast.58) | data formatting | bytes 6144000 | tf_op jit(solution)/shard_map/dot_general | solution.py:37
  21.1 5.1 %fusion.10 = f32[4,3,5120]{2,0,1:T(4,128)S(1)} fusion(f32[3,5120,50]{1,0,2:T(4,128)} %dot_general.36, s32[4]{0:T(128)S(1)} %copy-done.4), kind=kOutput, calls=%fused_computation.13 | convolution fusion | flops 36864200 | bytes 3317776 | tf_op jit(solution)/shard_map/dot_general | solution.py:37
  26.2 3.3 convert_reduce_fusion
  29.5 1.5 multiply_reduce_fusion
  31.0 6.3 %copy.30 = bf16[5120,384]{0,1:T(8,128)(2,1)} copy(bf16[5120,384]{1,0:T(8,128)(2,1)} %param.13) | data formatting | bytes 7864320 | tf_op args[4]
  37.4 5.6 %add_convert_fusion = bf16[4,128,5120]{2,1,0:T(8,128)(2,1)S(1)} fusion(bf16[4,128,5120]{2,1,0:T(8,128)(2,1)} %param.9, f32[4,5120]{1,0:T(4,128)S(1)} %get-tuple-element.6, f32[4,5120]{1,0:T(4,128)S(1)} %get-tuple-element.7, f32[4,128]{1,0:T(4,128)S(1)} %add_rsqrt_fusion.2, f32[4,128]{1,0:T(4,128)S(1)} %broadcast_multiply_fusion), kind=kLoop, calls=%fused_computation | loop fusion | flops 15728640 | bytes 10653696 | tf_op jit(solution)/shard_map/convert_element_type | solution.py:48
  43.0 2.2 multiply_reduce_fusion.1
  45.4 0.9 copy.31
  46.6 6.5 %convolution_convert_fusion = bf16[512,384]{1,0:T(8,128)(2,1)S(1)} fusion(bf16[512,5120]{1,0:T(8,128)(2,1)} %bitcast.59, bf16[5120,384]{1,0:T(8,128)(2,1)} %param.14), kind=kOutput, calls=%fused_computation.18 | convolution fusion | flops 2013462528 | bytes 9568256 | tf_op jit(solution)/shard_map/dot_general | solution.py:65
  54.1 6.4 %copy.29 = bf16[5120,384]{0,1:T(8,128)(2,1)} copy(bf16[5120,384]{1,0:T(8,128)(2,1)} %param.12) | data formatting | bytes 7864320 | tf_op args[3]
  60.5 5.5 %multiply_reduce_fusion.2 = (f32[4,128,3]{1,2,0:T(4,128)S(1)}, f32[4,128,3,128]{1,3,2,0:T(8,128)S(1)}) fusion(bf16[3,128,5120,1]{2,1,0,3:T(8,128)(2,1)} %bitcast.61, bf16[4,128,5120]{2,1,0:T(8,128)(2,1)} %copy-done), kind=kOutput, calls=%fused_computation.23 | convolution fusion | flops 2013657600 | bytes 9967616 | tf_op jit(solution)/shard_map/dot_general | solution.py:54
  66.4 45.1 %all-gather.5.cloned.1.call-done = bf16[64,128,3,128]{3,1,2,0:T(8,128)(2,1)} async-done(((bf16[4,128,3,128]{3,1,2,0:T(8,128)(2,1)}), bf16[64,128,3,128]{3,1,2,0:T(8,128)(2,1)}) %all-gather.5.cloned.1.call-update) | async-done | bytes 6291472 | tf_op jit(solution)/shard_map/all_gather | solution.py:70
  111.5 10.9 %fusion.29 = (f32[128,3,4]{2,1,0:T(4,128)S(1)}, f32[128,3,4,64]{3,2,1,0:T(4,128)S(1)}) fusion(bf16[4,128,3,128]{3,0,2,1:T(4,128)(2,1)S(1)} %copy.32, bf16[64,128,3,128]{3,1,2,0:T(8,128)(2,1)} %all-gather.5.cloned.1.call-done), kind=kOutput, calls=%fused_computation.40 | convolution fusion | flops 25360896 | bytes 7084032 | tf_op jit(solution)/shard_map/fphd,gphd->phfg/dot_general | solution.py:16
  122.4 1.1 fusion.20
  123.5 52.5 %all-gather.3.cloned.1.call-done = bf16[64,128,3,128]{3,1,2,0:T(8,128)(2,1)} async-done(((bf16[4,128,3,128]{3,1,2,0:T(8,128)(2,1)}), bf16[64,128,3,128]{3,1,2,0:T(8,128)(2,1)}) %all-gather.3.cloned.1.call-update) | async-done | bytes 6291472 | tf_op jit(solution)/shard_map/all_gather | solution.py:71
  176.0 12.7 %divide_convert_fusion = bf16[4,128,3,128]{3,0,2,1:T(4,128)(2,1)S(1)} fusion(bf16[64,128,3,128]{3,1,2,0:T(8,128)(2,1)} %all-gather.3.cloned.1.call-done, f32[128,3,4,64]{3,2,1,0:T(4,128)S(1)} %get-tuple-element.13, f32[4,128,3]{0,2,1:T(4,128)S(1)} %bitcast.63, f32[128,3,4]{2,1,0:T(4,128)S(1)} %get-tuple-element.12), kind=kOutput, calls=%fused_computation.24 | convolution fusion | flops 25755648 | bytes 7090176 | tf_op jit(solution)/shard_map/phfg,gphd->fphd/dot_general | solution.py:23
  189.0 7.7 %fusion.8 = f32[4,128,5120]{2,1,0:T(8,128)} fusion(bf16[4,128,384]{1,2,0:T(8,128)(2,1)S(1)} %bitcast.62, bf16[384,5120]{1,0:T(8,128)(2,1)} %param.15), kind=kOutput, calls=%fused_computation.11 | convolution fusion | flops 2013265920 | bytes 14811136 | tf_op jit(solution)/shard_map/dot_general | solution.py:74
  196.7 7.7 %convert_element_type.25 = f32[4,128,5120]{2,1,0:T(8,128)} convert(bf16[4,128,5120]{2,1,0:T(8,128)(2,1)} %param.9) | non-fusion elementwise | flops 2621440 | bytes 15728640 | tf_op jit(solution)/shard_map/convert_element_type | solution.py:43
  204.4 200.6 %reduce-scatter.2.cloned.1.call-done = f32[4,128,640]{2,1,0:T(8,128)} async-done(((f32[4,128,5120]{2,1,0:T(8,128)}), f32[4,128,640]{2,1,0:T(8,128)}) %reduce-scatter.2.cloned.1.call-update) | async-done | bytes 1310736 | tf_op jit(solution)/shard_map/reduce_scatter | solution.py:77
  405.0 1.9 add_convert_fusion.1
  407.0 13.6 %collective-permute-done = bf16[4,128,640]{2,1,0:T(8,128)(2,1)S(1)} collective-permute-done((bf16[4,128,640]{2,1,0:T(8,128)(2,1)S(1)}, bf16[4,128,640]{2,1,0:T(8,128)(2,1)S(1)}, u32[]{:S(2)}, u32[]{:S(2)}) %collective-permute-start) | collective-permute-done | bytes 655392 | tf_op jit(solution)/shard_map/ppermute | solution.py:12
  420.6 0.8 copy.57
  (35 shorter events, 3.0 us)
Async XLA Ops:
  6.5 105.0 %all-gather.5.cloned.1.call-start = ((), (), s32[]{:S(2)}) async-start(), calls=%async_computation.2 | async-start | bytes 6684672 | tf_op jit(solution)/shard_map/all_gather | solution.py:70
  15.2 5.9 %copy-start.4 = (s32[4]{0:T(128)S(1)}, s32[4]{0:T(128)}, u32[]{:S(2)}) copy-start(s32[4]{0:T(128)} %param.10) | copy-start | bytes 52
  15.2 14.3 %slice-start = ((s8[5242880]{0:T(1024)(128)(4,1)}), s8[1048576]{0:T(1024)(128)(4,1)S(1)}, s32[]{:S(2)}) async-start(s8[5242880]{0:T(1024)(128)(4,1)} %bitcast.55), calls=%async_computation.4 | async-start | bytes 2097152
  21.1 8.4 %slice-start.1 = ((s8[5242880]{0:T(1024)(128)(4,1)}), s8[4194304]{0:T(1024)(128)(4,1)S(1)}, s32[]{:S(2)}) async-start(s8[5242880]{0:T(1024)(128)(4,1)} %bitcast.55), calls=%async_computation.5 | async-start | bytes 8388608
  37.4 5.6 %copy-start.1 = (bf16[5120,384]{0,1:T(8,128)(2,1)S(1)}, bf16[5120,384]{0,1:T(8,128)(2,1)}, u32[]{:S(2)}) copy-start(bf16[5120,384]{0,1:T(8,128)(2,1)} %copy.30) | copy-start | bytes 11796484
  42.9 2.3 copy-start
  42.9 2.3 copy-start.2
  46.3 129.7 %all-gather.3.cloned.1.call-start = ((), (), s32[]{:S(2)}) async-start(), calls=%async_computation.1 | async-start | bytes 6684672 | tf_op jit(solution)/shard_map/all_gather | solution.py:71
  54.1 350.9 %reduce-scatter.2.cloned.1.call-start = ((), (), s32[]{:S(2)}) async-start(), calls=%async_computation.3 | async-start | bytes 11796480 | tf_op jit(solution)/shard_map/reduce_scatter | solution.py:77
  60.5 5.5 %copy-start.3 = (f32[384]{0:T(512)S(1)}, f32[384]{0:T(512)}, u32[]{:S(2)}) copy-start(f32[384]{0:T(512)} %param.16) | copy-start | bytes 4612
  406.9 13.7 %collective-permute-start = (bf16[4,128,640]{2,1,0:T(8,128)(2,1)S(1)}, bf16[4,128,640]{2,1,0:T(8,128)(2,1)S(1)}, u32[]{:S(2)}, u32[]{:S(2)}) collective-permute-start(bf16[4,128,640]{2,1,0:T(8,128)(2,1)S(1)} %add_convert_fusion.1), channel_id=1, source_target_pairs={{0,8},{8,16},{16,24},{24,32},{32,40},{40,48},{48,56},{56,64},{64,7... | collective-permute-start | bytes 1966088 | tf_op jit(solution)/shard_map/ppermute | solution.py:12
Sparse Core Ops, SparseCore 0:
  46.5 65.0 all-gather.4
  114.0 61.9 all-gather.2
  196.8 208.1 reduce-scatter.1
where the time goes:
time: 433 us; the launch traced here: 428 us
  waiting for transfers between devices  312 us (72%)
  matrix products  50.6 us (12%)
  local copies, waits for them, and re-layouts  30.5 us (7%)
  other arithmetic  21.2 us (5%)
  between operations  13.5 us (3%)
    reduce_scatter x1, waiting for transfers between devices, on_device(): lax.psum_scatter(partial_sum, 'head', scatter_dimension=2, tiled=True)  201 us
    all_gather x1, waiting for transfers between devices, on_device(): lax.all_gather(value_rows, 'frame', axis=0, tiled=True)  52.5 us
    all_gather x1, waiting for transfers between devices, on_device(): lax.all_gather(key_rows, 'frame', axis=0, tiled=True)  45.1 us
    unnamed x20, local copies, waits for them, and re-layouts  22.2 us
    ppermute x1, waiting for transfers between devices, shifted(): return lax.ppermute(value, axis, pairs)  13.6 us
    dot_general x1, matrix products, attend(): jnp.einsum('phfg,gphd->fphd', rounded, value_rows, preferred_element_type...  12.7 us
    dot_general x1, matrix products, attend(): jnp.einsum('fphd,gphd->phfg', queries, key_rows, preferred_element_type=j...  10.9 us
  transfers between devices with their start and end apart: 4, of which 4 were waited for; matrix products, arithmetic and copies ran while one was open for 9% of the time, Pallas kernels for 0%

commit v1 on v0

v1 whole, which is shorter than its diff:
```python
import functools

import jax
import jax.numpy as jnp
from jax import lax
from jax.experimental import pallas as pl
from jax.experimental.pallas import tpu as pltpu
from jax.sharding import PartitionSpec as P

HS = 128
EPS = 1e-06
MESH = pl.DeviceIdType.MESH
BF16, F32 = jnp.bfloat16, jnp.float32


def block_kernel(
    slots,
    ys,
    levels_ref,
    latents_hbm,
    table_hbm,
    wq_hbm,
    wk_hbm,
    wv_hbm,
    wo_hbm,
    qgain_ref,
    kgain_ref,
    out_ref,
    lat,
    table,
    modrows,
    hidden,
    weights,
    sent,
    got,
    attended,
    gathered,
    wout,
    psend,
    precv,
    pown,
    residual,
    gate_out,
    gate_in,
    load_sem,
    in_send,
    in_recv,
    back_send,
    back_recv,
    y_send,
    y_recv,
    w_send,
    w_recv,
    sib_send,
    sib_recv,
    x_send,
    x_recv,
    shift_send,
    shift_recv,
):
    frames, positions, width = lat.shape
    cols = sent.shape[2]
    heads = cols // HS
    rows = frames * positions
    chunk = rows // slots
    out_cols = width // (2 * ys)
    quarter = rows // 4
    me = lax.axis_index("frame")
    head = lax.axis_index("head")
    y, xlo = head // 2, head % 2
    core = me % 2
    sibling = me + 1 - 2 * core
    following = (me + 1) % slots
    half = cols // 2

    lat_parts = 4
    part = positions // lat_parts
    lat_loads = [
        pltpu.make_async_copy(
            latents_hbm.at[:, pl.ds(q * part, part), :],
            lat.at[:, pl.ds(q * part, part), :],
            load_sem.at[q],
        )
        for q in range(lat_parts)
    ]
    table_load = pltpu.make_async_copy(table_hbm, table, load_sem.at[4])
    weight_loads = [
        pltpu.make_async_copy(w_hbm, weights.at[t], load_sem.at[5 + t])
        for t, w_hbm in enumerate((wk_hbm, wv_hbm, wq_hbm))
    ]
    table_load.start()
    for load in lat_loads:
        load.start()
    for load in weight_loads:
        load.start()

    barrier = pltpu.get_barrier_semaphore()

    def greet(k, carry):
        pl.semaphore_signal(
            barrier, inc=1, device_id=((me + k) % slots, head), device_id_type=MESH
        )
        return carry

    lax.fori_loop(1, slots, greet, 0)
    for k in range(1, ys):
        pl.semaphore_signal(
            barrier, inc=1, device_id=(me, ((y + k) % ys) * 2 + xlo), device_id_type=MESH
        )
    pl.semaphore_signal(barrier, inc=1, device_id=(me, y * 2 + 1 - xlo), device_id_type=MESH)
    pl.semaphore_wait(barrier, slots - 1 + ys - 1 + 1)

    w_rows = pl.ds(pl.multiple_of(core * half, 64), half)
    w_copies = []
    for k in (1, ys - 1) + tuple(range(2, ys - 1)):
        peer = (y + k) % ys
        for s in range(2):
            copy = pltpu.make_async_remote_copy(
                src_ref=wo_hbm.at[w_rows, pl.ds(pl.multiple_of((peer * 2 + s) * out_cols, 128), out_cols)],
                dst_ref=wout.at[s, pl.ds(pl.multiple_of(y * cols + core * half, 64), half), :],
                send_sem=w_send.at[k - 1, s],
                recv_sem=w_recv.at[k - 1, s],
                device_id=(me, peer * 2 + xlo),
                device_id_type=MESH,
            )
            copy.start()
            w_copies.append((k, s, copy))
    own_w = []
    for s in range(2):
        copy = pltpu.make_async_copy(
            wo_hbm.at[:, pl.ds(pl.multiple_of((y * 2 + s) * out_cols, 128), out_cols)],
            wout.at[s, pl.ds(pl.multiple_of(y * cols, 128), cols), :],
            load_sem.at[8 + s],
        )
        copy.start()
        own_w.append(copy)

    table_load.wait()
    head_cols = pl.ds(pl.multiple_of(head * out_cols, 128), out_cols)
    for f in range(frames):
        level = levels_ref[f]
        modrows[f, 0] = jnp.broadcast_to(1.0 + table[level, 1:2, :], (8, width))
        modrows[f, 1] = jnp.broadcast_to(table[level, 0:1, :], (8, width))
        gate_out[f] = jnp.broadcast_to(table[level, 2:3, head_cols], (8, out_cols))

    shift_copies = [
        pltpu.make_async_remote_copy(
            src_ref=src,
            dst_ref=dst,
            send_sem=shift_send.at[n],
            recv_sem=shift_recv.at[n],
            device_id=(following, head),
            device_id_type=MESH,
        )
        for n, (src, dst) in enumerate(
            ((gate_out, gate_in), (latents_hbm.at[:, :, head_cols], residual))
        )
    ]

    step = 512

    def normalise(j, carry):
        low, high = [], []
        at = pl.ds(pl.multiple_of(j * 16, 16), 16)
        stats = []
        for f in range(frames):
            total = jnp.zeros((16, 128), F32)
            for c in range(0, width, 128):
                total += lat[f, at, c : c + 128].astype(F32)
            mean = jnp.sum(total, axis=-1, keepdims=True) * (1.0 / width)
            square = jnp.zeros((16, 128), F32)
            for c in range(0, width, 128):
                centred = lat[f, at, c : c + 128].astype(F32) - mean
                square += centred * centred
            var = jnp.sum(square, axis=-1, keepdims=True) * (1.0 / width)
            stats.append((mean, lax.rsqrt(var + EPS)))
        for c in range(0, width, step):
            at_c = slice(c, c + step)
            pieces = []
            for f in range(frames):
                mean, rstd = stats[f]
                scale = modrows[f, 0, :, at_c]
                offset = modrows[f, 1, :, at_c]
                normed = (lat[f, at, at_c].astype(F32) - mean) * rstd
                pieces.append((normed[:8] * scale + offset, normed[8:] * scale + offset))
            for side in range(2):
                for pair in range(frames // 2):
                    both = jnp.concatenate(
                        [pieces[2 * pair][side], pieces[2 * pair + 1][side]], axis=0
                    )
                    start = pl.multiple_of(j * 64 + side * 32 + pair * 16, 16)
                    hidden[pl.ds(start, 16), at_c] = both.astype(BF16)
        return carry

    per_part = part // 16
    for q in range(lat_parts):
        lat_loads[q].wait()
        lax.fori_loop(q * per_part, (q + 1) * per_part, normalise, 0)

    in_local = []
    for t in range(3):
        weight_loads[t].wait()
        projected = jnp.dot(hidden[...], weights[t], preferred_element_type=F32)
        for n in range(heads):
            at_n = slice(n * HS, (n + 1) * HS)
            one = projected[:, at_n]
            if t != 1:
                gain = (qgain_ref if t == 2 else kgain_ref)[:, at_n]
                power = jnp.mean(one * one, axis=-1, keepdims=True)
                one = one * lax.rsqrt(power + EPS) * gain
            sent[t, :, at_n] = one.astype(BF16)

        def send(k, carry):
            to = (me + k) % slots
            pltpu.make_async_remote_copy(
                src_ref=sent.at[t, pl.ds(pl.multiple_of(to * chunk, 32), chunk), :],
                dst_ref=got.at[t, pl.ds(pl.multiple_of(me * chunk, 32), chunk), :],
                send_sem=in_send.at[t],
                recv_sem=in_recv.at[t],
                device_id=(to, head),
                device_id_type=MESH,
            ).start()
            return carry

        lax.fori_loop(1, slots, send, 0)
        own = pl.ds(pl.multiple_of(me * chunk, 32), chunk)
        copy = pltpu.make_async_copy(sent.at[t, own, :], got.at[t, own, :], load_sem.at[10 + t])
        copy.start()
        in_local.append(copy)

    for copy in shift_copies:
        copy.start()

    for t in range(3):
        in_local[t].wait()
        others = got.at[t, pl.ds(0, rows - chunk), :]
        pltpu.make_async_copy(others, others, in_recv.at[t]).wait()

    per_slot = positions // slots
    row_at = lax.broadcasted_iota(jnp.int32, (per_slot, rows), 0)
    col_at = lax.broadcasted_iota(jnp.int32, (per_slot, rows), 1)
    bias = jnp.where(row_at == col_at % per_slot, 0.0, -1e9).astype(F32)
    q_rows = 256
    for n in range(heads):
        at_n = slice(n * HS, (n + 1) * HS)
        keys = got[0, :, at_n]
        values = jnp.concatenate([got[1, :, at_n], jnp.ones((rows, HS), BF16)], axis=1)
        for b in range(rows // q_rows):
            at_b = slice(b * q_rows, (b + 1) * q_rows)
            scores = lax.dot_general(
                got[2, at_b, at_n], keys, (((1,), (1,)), ((), ())), preferred_element_type=F32
            )
            scores = scores.reshape(q_rows // per_slot, per_slot, rows) + bias[None]
            largest = jnp.max(scores, axis=-1, keepdims=True)
            powers = jnp.exp((scores - largest) * (1.0 / HS**0.5))
            mixed = jnp.dot(
                powers.reshape(q_rows, rows).astype(BF16), values, preferred_element_type=F32
            )
            attended[at_b, at_n] = (mixed[:, :HS] / mixed[:, HS:]).astype(BF16)

    own_cols = pl.ds(pl.multiple_of(y * cols, 128), cols)
    arrive = gathered.at[pl.ds(pl.multiple_of(me * chunk, 32), chunk), own_cols]

    def send_back(k, carry):
        to = (me + k) % slots
        owner = (me + k + slots - 1) % slots
        pltpu.make_async_remote_copy(
            src_ref=attended.at[pl.ds(pl.multiple_of(owner * chunk, 32), chunk), :],
            dst_ref=arrive,
            send_sem=back_send,
            recv_sem=back_recv.at[me // (slots // 4)],
            device_id=(to, head),
            device_id_type=MESH,
        ).start()
        return carry

    lax.fori_loop(1, slots, send_back, 0)
    before = (me + slots - 1) % slots
    pltpu.make_async_copy(
        attended.at[pl.ds(pl.multiple_of(before * chunk, 32), chunk), :],
        arrive,
        back_recv.at[me // (slots // 4)],
    ).start()

    sib_copies = []
    for k, s, copy in w_copies:
        copy.wait()
        source = (y + ys - k) % ys
        piece = wout.at[s, pl.ds(pl.multiple_of(source * cols + core * half, 64), half), :]
        forward = pltpu.make_async_remote_copy(
            src_ref=piece,
            dst_ref=piece,
            send_sem=sib_send.at[k - 1, s],
            recv_sem=sib_recv.at[k - 1, s],
            device_id=(sibling, head),
            device_id_type=MESH,
        )
        forward.start()
        sib_copies.append(forward)

    y_copies = []
    for r in range(4):
        piece = gathered.at[pl.ds(r * quarter, quarter), own_cols]
        pltpu.make_async_copy(piece, piece, back_recv.at[r]).wait()
        for k in (1, ys - 1) + tuple(range(2, ys - 1)):
            copy = pltpu.make_async_remote_copy(
                src_ref=piece,
                dst_ref=piece,
                send_sem=y_send.at[r, k - 1],
                recv_sem=y_recv.at[r, k - 1],
                device_id=(me, ((y + k) % ys) * 2 + xlo),
                device_id_type=MESH,
            )
            copy.start()
            y_copies.append(copy)

    for copy in own_w + sib_copies:
        copy.wait()

    x_copies = []
    for r in range(4):
        at_r = slice(r * quarter, (r + 1) * quarter)
        for copy in y_copies[r * (ys - 1) : (r + 1) * (ys - 1)]:
            copy.wait()
        mixed = gathered[at_r, :]
        psend[at_r, :] = jnp.dot(mixed, wout[1 - xlo], preferred_element_type=F32).astype(BF16)
        copy = pltpu.make_async_remote_copy(
            src_ref=psend.at[pl.ds(r * quarter, quarter), :],
            dst_ref=precv.at[pl.ds(r * quarter, quarter), :],
            send_sem=x_send.at[r],
            recv_sem=x_recv.at[r],
            device_id=(me, y * 2 + 1 - xlo),
            device_id_type=MESH,
        )
        copy.start()
        x_copies.append(copy)
        pown[at_r, :] = jnp.dot(mixed, wout[xlo], preferred_element_type=F32)

    for copy in shift_copies:
        copy.wait()
    for r in range(4):
        x_copies[r].wait()
        for j in range(r * quarter // 64, (r + 1) * quarter // 64):
            at = slice(j * 16, (j + 1) * 16)
            total = pown[j * 64 : (j + 1) * 64, :] + precv[j * 64 : (j + 1) * 64, :].astype(F32)
            for f in range(frames):
                gate = gate_in[f]
                moved = jnp.concatenate(
                    [
                        total[f * 8 : (f + 1) * 8] * gate,
                        total[32 + f * 8 : 32 + (f + 1) * 8] * gate,
                    ],
                    axis=0,
                )
                out_ref[f, at, :] = (residual[f, at, :].astype(F32) + moved).astype(BF16)

    for t in range(3):
        others = sent.at[t, pl.ds(0, rows - chunk), :]
        pltpu.make_async_copy(others, others, in_send.at[t]).wait()
    others = attended.at[pl.ds(0, rows - chunk), :]
    pltpu.make_async_copy(others, others, back_send).wait()


def on_device(slots, ys, latents, levels, mod_table, wq, wk, wv, wo, qgain, kgain):
    frames, positions, width = latents.shape
    cols = wq.shape[1]
    rows = frames * positions
    out_cols = width // (2 * ys)
    vmem = pl.BlockSpec(memory_space=pltpu.VMEM)
    hbm = pl.BlockSpec(memory_space=pl.ANY)
    dma = pltpu.SemaphoreType.DMA
    return pl.pallas_call(
        functools.partial(block_kernel, slots, ys),
        out_shape=jax.ShapeDtypeStruct((frames, positions, out_cols), BF16),
        in_specs=[pl.BlockSpec(memory_space=pltpu.SMEM)] + [hbm] * 6 + [vmem] * 2,
        out_specs=vmem,
        scratch_shapes=[
            pltpu.VMEM((frames, positions, width), BF16),
            pltpu.VMEM(mod_table.shape, F32),
            pltpu.VMEM((frames, 2, 8, width), F32),
            pltpu.VMEM((rows, width), BF16),
            pltpu.VMEM((3, width, cols), BF16),
            pltpu.VMEM((3, rows, cols), BF16),
            pltpu.VMEM((3, rows, cols), BF16),
            pltpu.VMEM((rows, cols), BF16),
            pltpu.VMEM((rows, ys * cols), BF16),
            pltpu.VMEM((2, ys * cols, out_cols), BF16),
            pltpu.VMEM((rows, out_cols), BF16),
            pltpu.VMEM((rows, out_cols), BF16),
            pltpu.VMEM((rows, out_cols), F32),
            pltpu.VMEM((frames, positions, out_cols), BF16),
            pltpu.VMEM((frames, 8, out_cols), F32),
            pltpu.VMEM((frames, 8, out_cols), F32),
            dma((13,)),
            dma((3,)),
            dma((3,)),
            dma(()),
            dma((4,)),
            dma((4, ys - 1)),
            dma((4, ys - 1)),
            dma((ys - 1, 2)),
            dma((ys - 1, 2)),
            dma((ys - 1, 2)),
            dma((ys - 1, 2)),
            dma((4,)),
            dma((4,)),
            dma((2,)),
            dma((2,)),
        ],
        compiler_params=pltpu.CompilerParams(
            collective_id=0, has_side_effects=True, vmem_limit_bytes=60 << 20
        ),
        name="temporal_block",
    )(levels, latents, mod_table, wq, wk, wv, wo, qgain.reshape(1, cols), kgain.reshape(1, cols))


def solution(mesh):
    return jax.shard_map(
        functools.partial(on_device, mesh.shape["frame"], mesh.shape["head"] // 2),
        mesh=mesh,
        in_specs=(
            P("frame", None, None),
            P("frame"),
            P(),
            P(None, "head"),
            P(None, "head"),
            P(None, "head"),
            P("head", None),
            P("head"),
            P("head"),
        ),
        out_specs=P("frame", None, "head"),
        check_vma=False,
    )
```

time: 433 us -> 79.5 us (0.18)
  the two profiles are of different devices: /device:TPU:6 before, /device:TPU:64 now
where the time goes in v1:
time: 79.5 us; the launch traced here: 79.3 us
  Pallas kernels  68.8 us (87%)
  local copies, waits for them, and re-layouts  10.5 us (13%)
    pallas_call x1, Pallas kernels, on_device(): pl.pallas_call(functools.partial(block_kernel, slots, ys), out_shape=jax....  68.8 us
    unnamed x2, local copies, waits for them, and re-layouts  7.97 us

profile of v1, /device:TPU:64, one launch (start us, length us, event | category | flops | bytes accessed | tf_op | source)
XLA Modules:
  0.0 79.3 jit_solution(13529746214233293787)
XLA Ops:
  0.0 1.2 %reshape.6.qgain_ref = f32[1,384]{1,0:T(1,128)} reshape(f32[384]{0:T(512)} %param.16) | data formatting | bytes 3072 | tf_op jit(solution)/shard_map/reshape | solution.py:414
  1.2 1.3 %reshape.7.kgain_ref = f32[1,384]{1,0:T(1,128)} reshape(f32[384]{0:T(512)} %param.17) | data formatting | bytes 3072 | tf_op jit(solution)/shard_map/reshape | solution.py:414
  2.5 6.0 %copy.10.table_hbm = f32[50,3,5120]{2,1,0:T(4,128)} copy(f32[50,3,5120]{2,0,1:T(8,128)} %param.11) | data formatting | bytes 6144000 | tf_op args[2]
  8.5 68.8 %temporal_block.1 = bf16[4,128,640]{2,1,0:T(8,128)(2,1)} custom-call(s32[4]{0:T(128)} %levels_ref.1, bf16[4,128,5120]{2,1,0:T(8,128)(2,1)} %latents_hbm.1, f32[50,3,5120]{2,1,0:T(4,128)} %copy.10.table_hbm, bf16[5120,384]{1,0:T(8,128)(2,1)} %wq_hbm.1, bf16[5120,384]{1,0:T(8,128)(2,1)} %wk_hbm.1, bf16[5120,384]{1,0:T(8,128)(2,1)} %wv_hbm.1, ...), custom_call_target="tpu_custom_call" | custom-call | tf_op jit(solution)/shard_map/temporal_block/pallas_call | solution.py:372
  77.3 2.0 %copy.12 = bf16[4,128,640]{2,1,0:T(8,128)(2,1)} copy(bf16[4,128,640]{2,1,0:T(8,128)(2,1)} %temporal_block.1) | data formatting | bytes 1310720

commit v2 on v1

v2 whole, which is shorter than its diff:
```python
import functools

import jax
import jax.numpy as jnp
from jax import lax
from jax.experimental import pallas as pl
from jax.experimental.pallas import tpu as pltpu
from jax.sharding import PartitionSpec as P

HS = 128
EPS = 1e-06
MESH = pl.DeviceIdType.MESH
BF16, F32 = jnp.bfloat16, jnp.float32


def swap_halves(first, second):
    upper = lax.broadcasted_iota(jnp.int32, first.shape, 0) < 4
    return (
        jnp.where(upper, first, pltpu.roll(second, 4, 0)),
        jnp.where(upper, pltpu.roll(first, 4, 0), second),
    )


def block_kernel(
    slots,
    ys,
    levels_ref,
    latents_hbm,
    table_hbm,
    wq_hbm,
    wk_hbm,
    wv_hbm,
    wo_hbm,
    qgain_ref,
    kgain_ref,
    out_ref,
    lat,
    table,
    modrows,
    hidden,
    weights,
    sent,
    got,
    attended,
    gathered,
    wout,
    psend,
    precv,
    pown,
    residual,
    gate_out,
    gate_in,
    load_sem,
    in_send,
    in_recv,
    back_send,
    back_recv,
    y_send,
    y_recv,
    w_send,
    w_recv,
    sib_send,
    sib_recv,
    x_send,
    x_recv,
    shift_send,
    shift_recv,
):
    frames, positions, width = lat.shape
    cols = attended.shape[1]
    heads = cols // HS
    rows = frames * positions
    side = rows // 2
    chunk = side // slots
    out_cols = width // (2 * ys)
    quarter = rows // 4
    me = lax.axis_index("frame")
    head = lax.axis_index("head")
    y, xlo = head // 2, head % 2
    core = me % 2
    sibling = me + 1 - 2 * core
    following = (me + 1) % slots
    half = cols // 2

    def ring(steps):
        return (me, ((y + steps) % ys) * 2 + xlo)

    lat_parts = 4
    part = positions // lat_parts
    lat_loads = [
        pltpu.make_async_copy(
            latents_hbm.at[:, pl.ds(q * part, part), :],
            lat.at[:, pl.ds(q * part, part), :],
            load_sem.at[q],
        )
        for q in range(lat_parts)
    ]
    table_load = pltpu.make_async_copy(table_hbm, table, load_sem.at[4])
    weight_loads = [
        pltpu.make_async_copy(w_hbm, weights.at[t], load_sem.at[5 + t])
        for t, w_hbm in enumerate((wk_hbm, wv_hbm, wq_hbm))
    ]
    table_load.start()
    for load in lat_loads:
        load.start()

    barrier = pltpu.get_barrier_semaphore()

    def greet(k, carry):
        pl.semaphore_signal(
            barrier, inc=1, device_id=((me + k) % slots, head), device_id_type=MESH
        )
        return carry

    lax.fori_loop(1, slots, greet, 0)
    for k in range(1, ys):
        pl.semaphore_signal(barrier, inc=1, device_id=ring(k), device_id_type=MESH)
    pl.semaphore_signal(barrier, inc=1, device_id=(me, y * 2 + 1 - xlo), device_id_type=MESH)

    table_load.wait()
    head_cols = pl.ds(pl.multiple_of(head * out_cols, 128), out_cols)
    for f in range(frames):
        level = levels_ref[f]
        modrows[f, 0] = jnp.broadcast_to(1.0 + table[1, pl.ds(level, 1), :], (8, width))
        modrows[f, 1] = jnp.broadcast_to(table[0, pl.ds(level, 1), :], (8, width))
        gate_out[f] = jnp.broadcast_to(table[2, pl.ds(level, 1), head_cols], (8, out_cols))

    pl.semaphore_wait(barrier, slots - 1 + ys - 1 + 1)

    w_rows = pl.ds(pl.multiple_of(core * half, 64), half)
    w_copies = []
    for k in (2, 1, 3):
        peer = (y + k) % ys
        copy = pltpu.make_async_remote_copy(
            src_ref=wo_hbm.at[w_rows, pl.ds(pl.multiple_of(peer * 2 * out_cols, 128), 2 * out_cols)],
            dst_ref=wout.at[pl.ds(pl.multiple_of(y * cols + core * half, 64), half), :],
            send_sem=w_send.at[k - 1],
            recv_sem=w_recv.at[k - 1],
            device_id=ring(k),
            device_id_type=MESH,
        )
        copy.start()
        w_copies.append((k, copy))

    shift_copies = [
        pltpu.make_async_remote_copy(
            src_ref=src,
            dst_ref=dst,
            send_sem=shift_send.at[n],
            recv_sem=shift_recv.at[n],
            device_id=(following, head),
            device_id_type=MESH,
        )
        for n, (src, dst) in enumerate(
            ((gate_out, gate_in), (latents_hbm.at[:, :, head_cols], residual))
        )
    ]
    for copy in shift_copies:
        copy.start()
    for load in weight_loads:
        load.start()
    own_w = pltpu.make_async_copy(
        wo_hbm.at[:, pl.ds(pl.multiple_of(y * 2 * out_cols, 128), 2 * out_cols)],
        wout.at[pl.ds(pl.multiple_of(y * cols, 128), cols), :],
        load_sem.at[8],
    )
    own_w.start()

    step = 512

    def normalise(j, carry):
        at = pl.ds(pl.multiple_of(j * 16, 16), 16)
        stats = []
        for f in range(frames):
            total = jnp.zeros((16, 128), F32)
            for c in range(0, width, 128):
                total += lat[f, at, c : c + 128].astype(F32)
            mean = jnp.sum(total, axis=-1, keepdims=True) * (1.0 / width)
            square = jnp.zeros((16, 128), F32)
            for c in range(0, width, 128):
                centred = lat[f, at, c : c + 128].astype(F32) - mean
                square += centred * centred
            var = jnp.sum(square, axis=-1, keepdims=True) * (1.0 / width)
            stats.append((mean, lax.rsqrt(var + EPS)))
        for c in range(0, width, step):
            at_c = slice(c, c + step)
            pieces = []
            for f in range(frames):
                mean, rstd = stats[f]
                scale = modrows[f, 0, :, at_c]
                offset = modrows[f, 1, :, at_c]
                normed = (lat[f, at, at_c].astype(F32) - mean) * rstd
                pieces.append((normed[:8] * scale + offset, normed[8:] * scale + offset))
            for v in range(2):
                one = swap_halves(pieces[0][v], pieces[1][v])
                two = swap_halves(pieces[2][v], pieces[3][v])
                for s in range(2):
                    both = jnp.concatenate([one[s], two[s]], axis=0)
                    start = pl.multiple_of(j * 64 + v * 32 + s * 16, 16)
                    hidden[pl.ds(start, 16), at_c] = both.astype(BF16)
        return carry

    zs = slots // 4
    xhi, z = me // (2 * zs), (me // 2) % zs
    partners = []
    for across, along in ((1, 2), (0, 1), (1, 1), (0, 3), (1, 3), (0, 2), (1, 0)):
        chip = ((xhi + across) % 2) * 2 * zs + ((z + along) % zs) * 2
        partners += [chip + core, chip + 1 - core]
    partners.append(sibling)

    blocks = [(t, n) for t in range(3) for n in range(heads)]
    pairs = [blocks[b : b + 2] for b in range(0, len(blocks), 2)]
    sends = {0: (0, 2), 2: (2, 6), 4: (6, 9)}
    own = pl.ds(pl.multiple_of(me * chunk, 16), chunk)
    in_local = []

    def project(a):
        at_a = slice(a * side, (a + 1) * side)
        for b, pair in enumerate(pairs):
            if a == 0:
                for t, n in pair:
                    if n == 0:
                        weight_loads[t].wait()
            weight = jnp.concatenate(
                [weights[t, :, n * HS : (n + 1) * HS] for t, n in pair], axis=1
            )
            projected = jnp.dot(hidden[at_a, :], weight, preferred_element_type=F32)
            for m, (t, n) in enumerate(pair):
                one = projected[:, m * HS : (m + 1) * HS]
                if t != 1:
                    gain = (qgain_ref if t == 2 else kgain_ref)[n * HS : (n + 1) * HS]
                    power = jnp.mean(one * one, axis=-1, keepdims=True)
                    one = one * lax.rsqrt(power + EPS) * gain.reshape(1, HS)
                place = (t * heads + n) * HS
                sent[a, :, place : place + HS] = one.astype(BF16)
            if b in sends:
                first, last = sends[b]
                at_s = pl.ds(first * HS, (last - first) * HS)
                for to in partners:
                    pltpu.make_async_remote_copy(
                        src_ref=sent.at[a, pl.ds(pl.multiple_of(to * chunk, 16), chunk), at_s],
                        dst_ref=got.at[a, own, at_s],
                        send_sem=in_send.at[a],
                        recv_sem=in_recv.at[a],
                        device_id=(to, head),
                        device_id_type=MESH,
                    ).start()
        copy = pltpu.make_async_copy(sent.at[a, own, :], got.at[a, own, :], load_sem.at[9 + a])
        copy.start()
        in_local.append(copy)

    per_part = part // 16
    for a in range(2):
        for q in (2 * a, 2 * a + 1):
            lat_loads[q].wait()
            lax.fori_loop(q * per_part, (q + 1) * per_part, normalise, 0)
        project(a)

    per_slot = positions // slots // 2
    row_at = lax.broadcasted_iota(jnp.int32, (8, side), 0)
    col_at = lax.broadcasted_iota(jnp.int32, (8, side), 1)
    bias = jnp.where(row_at % per_slot == col_at % per_slot, 0.0, -1e9).astype(F32)
    own_cols = pl.ds(pl.multiple_of(y * cols, 128), cols)
    before = (me + slots - 1) % slots

    def attend(a):
        in_local[a].wait()
        others = got.at[a, pl.ds(0, side - chunk), :]
        pltpu.make_async_copy(others, others, in_recv.at[a]).wait()
        for n in range(heads):
            keys, values, queries = (
                got[a, :, (t * heads + n) * HS : (t * heads + n + 1) * HS] for t in range(3)
            )
            values = jnp.concatenate([values, jnp.ones((side, HS), BF16)], axis=1)
            scores = lax.dot_general(
                queries, keys, (((1,), (1,)), ((), ())), preferred_element_type=F32
            )
            scores = scores.reshape(side // 8, 8, side) + bias[None]
            largest = jnp.max(scores, axis=-1, keepdims=True)
            powers = jnp.exp((scores - largest) * (1.0 / HS**0.5))
            mixed = jnp.dot(
                powers.reshape(side, side).astype(BF16), values, preferred_element_type=F32
            )
            attended[a * side : (a + 1) * side, n * HS : (n + 1) * HS] = (
                mixed[:, :HS] / mixed[:, HS:]
            ).astype(BF16)

        arrive = gathered.at[pl.ds(pl.multiple_of(a * side + me * chunk, 16), chunk), own_cols]
        sem = back_recv.at[a * 2 + me // (slots // 2)]
        for to in partners:
            owner = (to + slots - 1) % slots
            pltpu.make_async_remote_copy(
                src_ref=attended.at[pl.ds(pl.multiple_of(a * side + owner * chunk, 16), chunk), :],
                dst_ref=arrive,
                send_sem=back_send.at[a],
                recv_sem=sem,
                device_id=(to, head),
                device_id_type=MESH,
            ).start()
        pltpu.make_async_copy(
            attended.at[pl.ds(pl.multiple_of(a * side + before * chunk, 16), chunk), :],
            arrive,
            sem,
        ).start()

    def y_copy(r, kind, steps, source, start, count):
        piece = gathered.at[
            pl.ds(r * quarter + start, count), pl.ds(pl.multiple_of(source * cols, 128), cols)
        ]
        copy = pltpu.make_async_remote_copy(
            src_ref=piece,
            dst_ref=piece,
            send_sem=y_send.at[r, kind],
            recv_sem=y_recv.at[r, kind],
            device_id=ring(steps),
            device_id_type=MESH,
        )
        copy.start()
        return copy

    y_first, y_second = {}, {}

    def spread(r):
        piece = gathered.at[pl.ds(r * quarter, quarter), own_cols]
        pltpu.make_async_copy(piece, piece, back_recv.at[r]).wait()
        y_first[r] = (y_copy(r, 0, 1, y, 0, quarter), y_copy(r, 1, ys - 1, y, 0, quarter))

    def forward(r):
        low, high = y_first[r]
        low.wait()
        one = y_copy(r, 2, 1, (y + ys - 1) % ys, 0, quarter // 2)
        high.wait()
        two = y_copy(r, 3, ys - 1, (y + 1) % ys, quarter // 2, quarter // 2)
        y_second[r] = (one, two)

    x_copies = []

    def combine(r):
        at_r = slice(r * quarter, (r + 1) * quarter)
        for copy in y_second[r]:
            copy.wait()
        partial = jnp.dot(gathered[at_r, :], wout[...], preferred_element_type=F32)
        lower, upper = partial[:, :out_cols], partial[:, out_cols:]
        psend[at_r, :] = jnp.where(xlo == 0, upper, lower).astype(BF16)
        copy = pltpu.make_async_remote_copy(
            src_ref=psend.at[pl.ds(r * quarter, quarter), :],
            dst_ref=precv.at[pl.ds(r * quarter, quarter), :],
            send_sem=x_send.at[r],
            recv_sem=x_recv.at[r],
            device_id=(me, y * 2 + 1 - xlo),
            device_id_type=MESH,
        )
        copy.start()
        x_copies.append(copy)
        pown[at_r, :] = jnp.where(xlo == 0, lower, upper)

    def finish(r):
        x_copies[r].wait()
        for j in range(r * quarter // 64, (r + 1) * quarter // 64):
            at = slice(j * 16, (j + 1) * 16)
            total = pown[j * 64 : (j + 1) * 64, :] + precv[j * 64 : (j + 1) * 64, :].astype(F32)
            moved = [[None, None] for _ in range(frames)]
            for v in range(2):
                for u in range(2):
                    start = v * 32 + u * 8
                    moved[2 * u][v], moved[2 * u + 1][v] = swap_halves(
                        total[start : start + 8], total[start + 16 : start + 24]
                    )
            for f in range(frames):
                added = jnp.concatenate([moved[f][0] * gate_in[f], moved[f][1] * gate_in[f]], axis=0)
                out_ref[f, at, :] = (residual[f, at, :].astype(F32) + added).astype(BF16)

    attend(0)
    spread(0)
    spread(1)
    attend(1)

    sib_copies = []
    for k, copy in w_copies:
        copy.wait()
        source = (y + ys - k) % ys
        piece = wout.at[pl.ds(pl.multiple_of(source * cols + core * half, 64), half), :]
        passed = pltpu.make_async_remote_copy(
            src_ref=piece,
            dst_ref=piece,
            send_sem=sib_send.at[k - 1],
            recv_sem=sib_recv.at[k - 1],
            device_id=(sibling, head),
            device_id_type=MESH,
        )
        passed.start()
        sib_copies.append(passed)

    forward(0)
    forward(1)
    spread(2)
    spread(3)
    for copy in [own_w] + sib_copies:
        copy.wait()
    combine(0)
    forward(2)
    combine(1)
    forward(3)
    combine(2)
    combine(3)
    for copy in shift_copies:
        copy.wait()
    for r in range(4):
        finish(r)

    for a in range(2):
        others = sent.at[a, pl.ds(0, side - chunk), :]
        pltpu.make_async_copy(others, others, in_send.at[a]).wait()
        others = attended.at[pl.ds(0, side - chunk), :]
        pltpu.make_async_copy(others, others, back_send.at[a]).wait()


def on_device(slots, ys, latents, levels, mod_table, wq, wk, wv, wo, qgain, kgain):
    frames, positions, width = latents.shape
    cols = wq.shape[1]
    rows = frames * positions
    out_cols = width // (2 * ys)
    vmem = pl.BlockSpec(memory_space=pltpu.VMEM)
    hbm = pl.BlockSpec(memory_space=pl.ANY)
    dma = pltpu.SemaphoreType.DMA
    return pl.pallas_call(
        functools.partial(block_kernel, slots, ys),
        out_shape=jax.ShapeDtypeStruct((frames, positions, out_cols), BF16),
        in_specs=[pl.BlockSpec(memory_space=pltpu.SMEM)] + [hbm] * 6 + [vmem] * 2,
        out_specs=vmem,
        scratch_shapes=[
            pltpu.VMEM((frames, positions, width), BF16),
            pltpu.VMEM((3, mod_table.shape[0], width), F32),
            pltpu.VMEM((frames, 2, 8, width), F32),
            pltpu.VMEM((rows, width), BF16),
            pltpu.VMEM((3, width, cols), BF16),
            pltpu.VMEM((2, rows // 2, 3 * cols), BF16),
            pltpu.VMEM((2, rows // 2, 3 * cols), BF16),
            pltpu.VMEM((rows, cols), BF16),
            pltpu.VMEM((rows, ys * cols), BF16),
            pltpu.VMEM((ys * cols, 2 * out_cols), BF16),
            pltpu.VMEM((rows, out_cols), BF16),
            pltpu.VMEM((rows, out_cols), BF16),
            pltpu.VMEM((rows, out_cols), F32),
            pltpu.VMEM((frames, positions, out_cols), BF16),
            pltpu.VMEM((frames, 8, out_cols), F32),
            pltpu.VMEM((frames, 8, out_cols), F32),
            dma((11,)),
            dma((2,)),
            dma((2,)),
            dma((2,)),
            dma((4,)),
            dma((4, 4)),
            dma((4, 4)),
            dma((ys - 1,)),
            dma((ys - 1,)),
            dma((ys - 1,)),
            dma((ys - 1,)),
            dma((4,)),
            dma((4,)),
            dma((2,)),
            dma((2,)),
        ],
        compiler_params=pltpu.CompilerParams(
            collective_id=0, has_side_effects=True, vmem_limit_bytes=60 << 20
        ),
        name="temporal_block",
    )(levels, latents, jnp.transpose(mod_table, (1, 0, 2)), wq, wk, wv, wo, qgain, kgain)


def solution(mesh):
    return jax.shard_map(
        functools.partial(on_device, mesh.shape["frame"], mesh.shape["head"] // 2),
        mesh=mesh,
        in_specs=(
            P("frame", None, None),
            P("frame"),
            P(),
            P(None, "head"),
            P(None, "head"),
            P(None, "head"),
            P("head", None),
            P("head"),
            P("head"),
        ),
        out_specs=P("frame", None, "head"),
        check_vma=False,
    )
```

time: 79.5 us -> 61.9 us (0.78)
  the two profiles are of different devices: /device:TPU:64 before, /device:TPU:6 now
where the time goes in v2:
time: 61.9 us; the launch traced here: 61.7 us
  Pallas kernels  59.7 us (96%)
  local copies, waits for them, and re-layouts  1.98 us (3%)
    pallas_call x1, Pallas kernels, on_device(): pl.pallas_call(functools.partial(block_kernel, slots, ys), out_shape=jax....  59.7 us
    unnamed x1, local copies, waits for them, and re-layouts  1.98 us

profile of v2, /device:TPU:6, one launch (start us, length us, event | category | flops | bytes accessed | tf_op | source)
XLA Modules:
  0.0 61.7 jit_solution(7751313014613665447)
XLA Ops:
  0.0 59.7 %temporal_block.1 = bf16[4,128,640]{2,1,0:T(8,128)(2,1)} custom-call(s32[4]{0:T(128)} %levels_ref.1, bf16[4,128,5120]{2,1,0:T(8,128)(2,1)} %latents_hbm.1, f32[3,50,5120]{2,1,0:T(8,128)} %bitcast.1, bf16[5120,384]{1,0:T(8,128)(2,1)} %wq_hbm.1, bf16[5120,384]{1,0:T(8,128)(2,1)} %wk_hbm.1, bf16[5120,384]{1,0:T(8,128)(2,1)} %wv_hbm.1, ...), custom_call_target="tpu_custom_call" | custom-call | tf_op jit(solution)/shard_map/temporal_block/pallas_call | solution.py:426
  59.7 2.0 %copy.11 = bf16[4,128,640]{2,1,0:T(8,128)(2,1)} copy(bf16[4,128,640]{2,1,0:T(8,128)(2,1)} %temporal_block.1) | data formatting | bytes 1310720

commit v3 on v2

--- a/solution.py
+++ b/solution.py
@@ -203,7 +203,7 @@
     zs = slots // 4
     xhi, z = me // (2 * zs), (me // 2) % zs
     partners = []
-    for across, along in ((1, 2), (0, 1), (1, 1), (0, 3), (1, 3), (0, 2), (1, 0)):
+    for across, along in ((1, 2), (1, 1), (1, 3), (1, 0), (0, 2), (0, 1), (0, 3)):
         chip = ((xhi + across) % 2) * 2 * zs + ((z + along) % zs) * 2
         partners += [chip + core, chip + 1 - core]
     partners.append(sibling)

time: 61.9 us -> 62.1 us (level)
  no operation moved by 1% of the time
where the time goes in v3:
time: 62.1 us; the launch traced here: 61.5 us
  Pallas kernels  59.6 us (96%)
  local copies, waits for them, and re-layouts  1.98 us (3%)
    pallas_call x1, Pallas kernels, on_device(): pl.pallas_call(functools.partial(block_kernel, slots, ys), out_shape=jax....  59.6 us
    unnamed x1, local copies, waits for them, and re-layouts  1.98 us

profile of v3, /device:TPU:6, one launch (start us, length us, event | category | flops | bytes accessed | tf_op | source)
XLA Modules:
  0.0 61.5 jit_solution(10901430951379450039)
XLA Ops:
  0.0 59.6 %temporal_block.1 = bf16[4,128,640]{2,1,0:T(8,128)(2,1)} custom-call(s32[4]{0:T(128)} %levels_ref.1, bf16[4,128,5120]{2,1,0:T(8,128)(2,1)} %latents_hbm.1, f32[3,50,5120]{2,1,0:T(8,128)} %bitcast.1, bf16[5120,384]{1,0:T(8,128)(2,1)} %wq_hbm.1, bf16[5120,384]{1,0:T(8,128)(2,1)} %wk_hbm.1, bf16[5120,384]{1,0:T(8,128)(2,1)} %wv_hbm.1, ...), custom_call_target="tpu_custom_call" | custom-call | tf_op jit(solution)/shard_map/temporal_block/pallas_call | solution.py:426
  59.6 2.0 %copy.11 = bf16[4,128,640]{2,1,0:T(8,128)(2,1)} copy(bf16[4,128,640]{2,1,0:T(8,128)(2,1)} %temporal_block.1) | data formatting | bytes 1310720
